TPU v7x, 256 devices: a whole 4x4x8 slice. The times are simulated.
256 devices in a mesh: row: 8 (over y, x_hi), phi: 32 (over x_lo, z, core).
Axes of the slice: x: 4 (x_hi: 2, x_lo: 2; x = x_hi * 2 + x_lo), y: 4, z: 8, core: 2. Of those that a mesh axis runs over, the one named last changes fastest.
Arguments:
- density: float32 [32, 16, 8192], P('row', None, 'phi'), may hold values from 0.5 to 2
- momentum: float32 [3, 32, 16, 8192], P(None, 'row', None, 'phi'), may hold values from -3 to 3
- field: float32 [3, 32, 16, 8192], P(None, 'row', None, 'phi'), may hold values from -3 to 3
- shift: int32 [32], P('row'), may hold values from 0 to 8191
- frac: float32 [32], P('row'), may hold values from 0 to 1
Outputs:
- density_next: float32 [32, 16, 8192], P('row', None, 'phi')
- momentum_next: float32 [3, 32, 16, 8192], P(None, 'row', None, 'phi')
- field_next: float32 [3, 32, 16, 8192], P(None, 'row', None, 'phi')
Inputs may be any that keep to these rules, and one draw needn't show every extreme that they name: The shift of a radial column applies to every vertical and azimuthal cell of that column.
All inputs are finite; a program needn't handle non-finite values.
Results may differ from a plain program's by a relative error of at most 0.00002.
Values sent between devices are 32-bit elements; how exact they have to be, the bound alone decides.
A program may use at most 64 MiB of HBM per device.

v0:
```python
import jax
import jax.numpy as jnp
from jax import lax
from jax.sharding import PartitionSpec as P

TIME_STEP = 0.025
SOUND_SQUARED = 1.0
ORBIT_FREQ = 1.0
SHEAR_RATE = 1.5
NORMAL_AXES = (0, 2, 1)


def with_halo(block, sides, width):
    for axis, dim in sides:
        count = lax.axis_size(axis)
        forward = [(i, i + 1) for i in range(count - 1)]
        forward.append((count - 1, 0))
        backward = [(target, source) for source, target in forward]
        low = lax.ppermute(
            lax.slice_in_dim(block, block.shape[dim] - width, None, axis=dim), axis, forward
        )
        high = lax.ppermute(lax.slice_in_dim(block, 0, width, axis=dim), axis, backward)
        block = jnp.concatenate([low, block, high], axis=dim)
    return block


def passed_along(block, axis, distance):
    devices = range(lax.axis_size(axis))
    route = [((i - distance) % len(devices), i) for i in devices]
    return lax.ppermute(block, axis, route)


def from_lower(values, axis_dim):
    return jnp.roll(values, 1, axis_dim)


def from_upper(values, axis_dim):
    return jnp.roll(values, -1, axis_dim)


def exit_update(values, fraction, axis_dim):
    upcoming = jnp.roll(values, -1, axis_dim)
    previous = jnp.roll(values, 1, axis_dim)
    further = jnp.roll(values, -2, axis_dim)
    interface = 7.0 / 12.0 * (values + upcoming) - 1.0 / 12.0 * (previous + further)
    interface = jnp.clip(interface, jnp.minimum(values, upcoming), jnp.maximum(values, upcoming))
    left_face = jnp.roll(interface, 1, axis_dim)
    curvature = 6.0 * (values - 0.5 * (interface + left_face))
    outgoing = fraction * (
        interface
        - 0.5 * fraction * (interface - left_face - (1.0 - 2.0 / 3.0 * fraction) * curvature)
    )
    return values - outgoing + jnp.roll(outgoing, 1, axis_dim)


def face_flux(density, momenta, normal_field, centred, normal_dir):
    axis_dim = NORMAL_AXES[normal_dir]

    def state_of(picker):
        fields = [picker(entry) for entry in centred]
        fields[normal_dir] = normal_field
        return (picker(density), [picker(entry) for entry in momenta], fields)

    lower_state = state_of(lambda values: from_lower(values, axis_dim))
    upper_state = state_of(lambda values: values)

    def physical(state):
        dens, moms, fields = state
        veloc = [entry / dens for entry in moms]
        magnetic = 0.5 * (fields[0] * fields[0] + fields[1] * fields[1] + fields[2] * fields[2])
        flux_moms = [
            moms[comp] * veloc[normal_dir] - fields[normal_dir] * fields[comp] for comp in range(3)
        ]
        flux_moms[normal_dir] = flux_moms[normal_dir] + (dens * SOUND_SQUARED + magnetic)
        flux_fields = [
            fields[comp] * veloc[normal_dir] - fields[normal_dir] * veloc[comp] for comp in range(3)
        ]
        speed = jnp.abs(veloc[normal_dir]) + jnp.sqrt(SOUND_SQUARED + 2.0 * magnetic / dens)
        return (moms[normal_dir], flux_moms, flux_fields, speed)

    lower_flux = physical(lower_state)
    upper_flux = physical(upper_state)
    fastest = jnp.maximum(lower_flux[3], upper_flux[3])

    def blend(flux_low, flux_up, cons_low, cons_up):
        return 0.5 * (flux_low + flux_up) - 0.5 * fastest * (cons_up - cons_low)

    mass = blend(lower_flux[0], upper_flux[0], lower_state[0], upper_state[0])
    moms = [
        blend(lower_flux[1][comp], upper_flux[1][comp], lower_state[1][comp], upper_state[1][comp])
        for comp in range(3)
    ]
    fields = [
        blend(lower_flux[2][comp], upper_flux[2][comp], lower_state[2][comp], upper_state[2][comp])
        for comp in range(3)
    ]
    return (mass, moms, fields)


def godunov(extended):
    density = extended[0]
    momenta = [extended[1], extended[2], extended[3]]
    faces = [extended[4], extended[5], extended[6]]
    centred = [
        0.5 * (faces[comp] + from_upper(faces[comp], NORMAL_AXES[comp])) for comp in range(3)
    ]
    fluxes = [face_flux(density, momenta, faces[direc], centred, direc) for direc in range(3)]
    edge_z = 0.25 * (
        -fluxes[0][2][1]
        - from_lower(fluxes[0][2][1], 2)
        + fluxes[1][2][0]
        + from_lower(fluxes[1][2][0], 0)
    )
    edge_y = 0.25 * (
        fluxes[0][2][2]
        + from_lower(fluxes[0][2][2], 1)
        - fluxes[2][2][0]
        - from_lower(fluxes[2][2][0], 0)
    )
    edge_x = 0.25 * (
        -fluxes[1][2][2]
        - from_lower(fluxes[1][2][2], 1)
        + fluxes[2][2][1]
        + from_lower(fluxes[2][2][1], 2)
    )

    def rise(values, axis_dim):
        return from_upper(values, axis_dim) - values

    field_x = faces[0] - TIME_STEP * (rise(edge_z, 2) - rise(edge_y, 1))
    field_y = faces[1] - TIME_STEP * (rise(edge_x, 1) - rise(edge_z, 0))
    field_z = faces[2] - TIME_STEP * (rise(edge_y, 0) - rise(edge_x, 2))

    def divergence(pieces):
        total = rise(pieces[0], NORMAL_AXES[0])
        total = total + rise(pieces[1], NORMAL_AXES[1])
        return total + rise(pieces[2], NORMAL_AXES[2])

    new_density = density - TIME_STEP * divergence([fluxes[direc][0] for direc in range(3)])
    new_moms = [
        momenta[comp] - TIME_STEP * divergence([fluxes[direc][1][comp] for direc in range(3)])
        for comp in range(3)
    ]
    new_moms[0] = new_moms[0] + TIME_STEP * 2.0 * ORBIT_FREQ * momenta[1]
    new_moms[1] = new_moms[1] - TIME_STEP * (2.0 - SHEAR_RATE) * ORBIT_FREQ * momenta[0]
    stacked = jnp.stack(
        [new_density, new_moms[0], new_moms[1], new_moms[2], field_x, field_y, field_z]
    )
    return stacked[:, 2:-2, :, 2:-2]


def body(density, momentum, field, shift, frac):
    fields_all = jnp.concatenate([density[None], momentum, field], 0)
    block_cells = fields_all.shape[3]
    widened = with_halo(fields_all, (("phi", 3),), 3)
    exited = exit_update(widened, frac[None, :, None, None], 3)[:, :, :, 3:-3]
    block_steps = shift // block_cells
    within = shift % block_cells
    current = exited
    for exponent in range(lax.axis_size("phi").bit_length() - 1):
        moved_block = passed_along(current, "phi", 1 << exponent)
        chosen = block_steps >> exponent & 1 == 1
        current = jnp.where(chosen[None, :, None, None], moved_block, current)
    lower_block = passed_along(current, "phi", 1)
    joined = jnp.concatenate([lower_block, current], 3)

    def column_slice(piece, start):
        return lax.dynamic_slice_in_dim(piece, start, block_cells, 2)

    starts = block_cells - within
    remapped = jax.vmap(column_slice, in_axes=(1, 0), out_axes=1)(joined, starts)
    widened_state = with_halo(remapped, (("row", 1), ("phi", 3)), 2)
    result = godunov(widened_state)
    return (result[0], result[1:4], result[4:7])


def solution(mesh):
    return jax.shard_map(
        body,
        mesh=mesh,
        in_specs=(
            P("row", None, "phi"),
            P(None, "row", None, "phi"),
            P(None, "row", None, "phi"),
            P("row"),
            P("row"),
        ),
        out_specs=(P("row", None, "phi"), P(None, "row", None, "phi"), P(None, "row", None, "phi")),
        check_vma=False,
    )
```

profile of v0, /device:TPU:65, one launch (start us, length us, event | category | flops | bytes accessed | tf_op | source)
XLA Modules:
  0.0 174.3 jit_solution(16750747550559745747)
XLA Ops:
  0.7 1.1 pad_maximum_fusion.7
  1.9 2.3 %collective-permute-start = (f32[7,4,16,3]{3,2,1,0:T(8,128)S(1)}, f32[7,4,16,3]{3,2,1,0:T(8,128)S(1)}, u32[]{:S(2)}, u32[]{:S(2)}) collective-permute-start(f32[7,4,16,3]{3,2,1,0:T(8,128)S(1)} %get-tuple-element.89), channel_id=1, source_target_pairs={{0,1},{1,2},{2,3},{3,4},{4,5},{5,6},{6,7},{7,8},{8,9},{9,10},{10,1... | collective-permute-start | bytes 16136 | tf_op jit(solution)/shard_map/ppermute | solution.py:19
  4.2 3.0 %collective-permute-done = f32[7,4,16,3]{3,2,1,0:T(8,128)S(1)} collective-permute-done((f32[7,4,16,3]{3,2,1,0:T(8,128)S(1)}, f32[7,4,16,3]{3,2,1,0:T(8,128)S(1)}, u32[]{:S(2)}, u32[]{:S(2)}) %collective-permute-start) | collective-permute-done | bytes 5408 | tf_op jit(solution)/shard_map/ppermute | solution.py:19
  7.2 2.5 %collective-permute-done.1 = f32[7,4,16,3]{3,2,1,0:T(8,128)S(1)} collective-permute-done((f32[7,4,16,3]{3,2,1,0:T(8,128)S(1)}, f32[7,4,16,3]{3,2,1,0:T(8,128)S(1)}, u32[]{:S(2)}, u32[]{:S(2)}) %collective-permute-start.1) | collective-permute-done | bytes 5408 | tf_op jit(solution)/shard_map/ppermute | solution.py:22
  10.6 0.6 fusion.3
  12.6 5.4 %collective-permute-done.2 = f32[7,4,16,256]{3,2,1,0:T(8,128)S(1)} collective-permute-done((f32[7,4,16,256]{3,2,1,0:T(8,128)S(1)}, f32[7,4,16,256]{3,2,1,0:T(8,128)S(1)}, u32[]{:S(2)}, u32[]{:S(2)}) %collective-permute-start.2) | collective-permute-done | bytes 458784 | tf_op jit(solution)/shard_map/ppermute | solution.py:30
  18.1 4.1 %collective-permute-start.3 = (f32[7,4,16,256]{3,2,1,0:T(8,128)S(1)}, f32[7,4,16,256]{3,2,1,0:T(8,128)S(1)}, u32[]{:S(2)}, u32[]{:S(2)}) collective-permute-start(f32[7,4,16,256]{3,2,1,0:T(8,128)S(1)} %broadcast_select_fusion), channel_id=1, source_target_pairs={{30,0},{31,1},{0,2},{1,3},{2,4},{3,5},{4,6},{5,7},{6,8},{7,9},{8,1... | collective-permute-start | bytes 1376264 | tf_op jit(solution)/shard_map/ppermute | solution.py:30
  22.3 9.3 %collective-permute-done.3 = f32[7,4,16,256]{3,2,1,0:T(8,128)S(1)} collective-permute-done((f32[7,4,16,256]{3,2,1,0:T(8,128)S(1)}, f32[7,4,16,256]{3,2,1,0:T(8,128)S(1)}, u32[]{:S(2)}, u32[]{:S(2)}) %collective-permute-start.3) | collective-permute-done | bytes 458784 | tf_op jit(solution)/shard_map/ppermute | solution.py:30
  31.8 12.6 %collective-permute-done.4 = f32[7,4,16,256]{3,2,1,0:T(8,128)S(1)} collective-permute-done((f32[7,4,16,256]{3,2,1,0:T(8,128)S(1)}, f32[7,4,16,256]{3,2,1,0:T(8,128)S(1)}, u32[]{:S(2)}, u32[]{:S(2)}) %collective-permute-start.4) | collective-permute-done | bytes 458784 | tf_op jit(solution)/shard_map/ppermute | solution.py:30
  44.6 23.2 %collective-permute-done.5 = f32[7,4,16,256]{3,2,1,0:T(8,128)S(1)} collective-permute-done((f32[7,4,16,256]{3,2,1,0:T(8,128)S(1)}, f32[7,4,16,256]{3,2,1,0:T(8,128)S(1)}, u32[]{:S(2)}, u32[]{:S(2)}) %collective-permute-start.5) | collective-permute-done | bytes 458784 | tf_op jit(solution)/shard_map/ppermute | solution.py:30
  68.0 0.6 collective-permute-start.6
  68.6 9.8 %collective-permute-done.6 = f32[7,4,16,256]{3,2,1,0:T(8,128)S(1)} collective-permute-done((f32[7,4,16,256]{3,2,1,0:T(8,128)S(1)}, f32[7,4,16,256]{3,2,1,0:T(8,128)S(1)}, u32[]{:S(2)}, u32[]{:S(2)}) %collective-permute-start.6) | collective-permute-done | bytes 458784 | tf_op jit(solution)/shard_map/ppermute | solution.py:30
  78.5 27.7 %collective-permute-start.7 = (f32[7,4,16,256]{3,2,1,0:T(8,128)S(1)}, f32[7,4,16,256]{3,2,1,0:T(8,128)S(1)}, u32[]{:S(2)}, u32[]{:S(2)}) collective-permute-start(f32[7,4,16,256]{3,2,1,0:T(8,128)S(1)} %broadcast_select_fusion.4), channel_id=1, source_target_pairs={{31,0},{0,1},{1,2},{2,3},{3,4},{4,5},{5,6},{6,7},{7,8},{8,9},{9,10... | collective-permute-start | bytes 1376264 | tf_op jit(solution)/shard_map/ppermute | solution.py:30
  106.3 5.4 %collective-permute-done.7 = f32[7,4,16,256]{3,2,1,0:T(8,128)S(1)} collective-permute-done((f32[7,4,16,256]{3,2,1,0:T(8,128)S(1)}, f32[7,4,16,256]{3,2,1,0:T(8,128)S(1)}, u32[]{:S(2)}, u32[]{:S(2)}) %collective-permute-start.7) | collective-permute-done | bytes 458784 | tf_op jit(solution)/shard_map/ppermute | solution.py:30
  111.8 7.5 %copy.868 = f32[7,4,16,512]{2,0,1,3:T(8,128)} copy(f32[7,4,16,512]{3,2,1,0:T(8,128)S(1)} %pad_maximum_fusion.1) | data formatting | bytes 1835008 | tf_op jit(solution)/shard_map/concatenate | solution.py:165
  119.3 6.6 %gather_fusion = f32[4,7,16,256]{2,1,3,0:T(8,128)} fusion(f32[4,7,16,512]{2,1,0,3:T(8,128)} %bitcast.359, s32[4]{0:T(128)S(1)} %fusion.87), kind=kCustom, calls=%fused_computation | custom fusion | bytes 917568 | tf_op jit(solution)/shard_map/vmap()/gather | solution.py:168
  125.9 3.8 %fusion.95 = (f32[7,2,16,256]{2,0,3,1:T(8,128)}, f32[7,2,16,256]{2,0,3,1:T(8,128)S(1)}) fusion(f32[7,4,16,256]{2,0,3,1:T(8,128)} %bitcast.357), kind=kLoop, calls=%fused_computation.343 | loop fusion | bytes 917504 | tf_op jit(solution)/shard_map/slice | solution.py:20
  129.7 2.1 %copy.869 = f32[7,2,16,256]{3,2,1,0:T(8,128)S(1)} copy(f32[7,2,16,256]{2,0,3,1:T(8,128)} %get-tuple-element.45) | data formatting | bytes 458752 | tf_op jit(solution)/shard_map/slice | solution.py:20
  131.8 0.6 copy.870
  132.4 5.2 %collective-permute-start.9 = (f32[7,2,16,256]{3,2,1,0:T(8,128)S(1)}, f32[7,2,16,256]{3,2,1,0:T(8,128)S(1)}, u32[]{:S(2)}, u32[]{:S(2)}) collective-permute-start(f32[7,2,16,256]{3,2,1,0:T(8,128)S(1)} %copy.870), channel_id=1, source_target_pairs={{32,0},{64,32},{96,64},{128,96},{160,128},{192,160},{224,192},{0,2... | collective-permute-start | bytes 688136 | tf_op jit(solution)/shard_map/ppermute | solution.py:22
  137.6 2.7 %copy.871 = f32[7,4,16,256]{3,2,1,0:T(8,128)S(1)} copy(f32[7,4,16,256]{2,0,3,1:T(8,128)} %bitcast.358) | data formatting | bytes 917504 | tf_op jit(solution)/shard_map/vmap()/transpose | solution.py:171
  140.6 5.5 %collective-permute-done.8 = f32[7,2,16,256]{3,2,1,0:T(8,128)S(1)} collective-permute-done((f32[7,2,16,256]{3,2,1,0:T(8,128)S(1)}, f32[7,2,16,256]{3,2,1,0:T(8,128)S(1)}, u32[]{:S(2)}, u32[]{:S(2)}) %collective-permute-start.8) | collective-permute-done | bytes 229408 | tf_op jit(solution)/shard_map/ppermute | solution.py:19
  146.4 4.0 %collective-permute-start.10 = (f32[7,8,16,2]{3,2,1,0:T(8,128)S(1)}, f32[7,8,16,2]{3,2,1,0:T(8,128)S(1)}, u32[]{:S(2)}, u32[]{:S(2)}) collective-permute-start(f32[7,8,16,2]{3,2,1,0:T(8,128)S(1)} %get-tuple-element.85), channel_id=1, source_target_pairs={{0,1},{1,2},{2,3},{3,4},{4,5},{5,6},{6,7},{7,8},{8,9},{9,10},{10,1... | collective-permute-start | bytes 21512 | tf_op jit(solution)/shard_map/ppermute | solution.py:19
  150.4 5.4 %collective-permute-done.10 = f32[7,8,16,2]{3,2,1,0:T(8,128)S(1)} collective-permute-done((f32[7,8,16,2]{3,2,1,0:T(8,128)S(1)}, f32[7,8,16,2]{3,2,1,0:T(8,128)S(1)}, u32[]{:S(2)}, u32[]{:S(2)}) %collective-permute-start.10) | collective-permute-done | bytes 7200 | tf_op jit(solution)/shard_map/ppermute | solution.py:19
  155.8 2.5 %collective-permute-done.11 = f32[7,8,16,2]{3,2,1,0:T(8,128)S(1)} collective-permute-done((f32[7,8,16,2]{3,2,1,0:T(8,128)S(1)}, f32[7,8,16,2]{3,2,1,0:T(8,128)S(1)}, u32[]{:S(2)}, u32[]{:S(2)}) %collective-permute-start.11) | collective-permute-done | bytes 7200 | tf_op jit(solution)/shard_map/ppermute | solution.py:22
  167.3 1.7 fusion.30
  169.0 0.7 fusion.15
  169.7 0.7 fusion.24
  170.3 0.7 fusion.20
  171.0 0.8 pad_maximum_fusion.10
  172.6 0.8 pad_maximum_fusion.8
  173.4 0.9 fusion.76
  (142 shorter events, 12.9 us)
Async XLA Ops:
  0.6 9.0 %copy-start = (f32[3,4,16,256]{3,2,1,0:T(8,128)S(1)}, f32[3,4,16,256]{3,2,1,0:T(8,128)}, u32[]{:S(2)}) copy-start(f32[3,4,16,256]{3,2,1,0:T(8,128)} %param.7) | copy-start | bytes 589828
  0.6 9.0 %copy-start.1 = (f32[3,4,16,256]{3,2,1,0:T(8,128)S(1)}, f32[3,4,16,256]{3,2,1,0:T(8,128)}, u32[]{:S(2)}) copy-start(f32[3,4,16,256]{3,2,1,0:T(8,128)} %param.6) | copy-start | bytes 589828
  0.7 9.0 %copy-start.2 = (f32[4,16,256]{2,1,0:T(8,128)S(1)}, f32[4,16,256]{2,1,0:T(8,128)}, u32[]{:S(2)}) copy-start(f32[4,16,256]{2,1,0:T(8,128)} %param.5) | copy-start | bytes 196612
  0.7 3.5 %copy-start.3 = (f32[4]{0:T(128)S(1)}, f32[4]{0:T(128)}, u32[]{:S(2)}) copy-start(f32[4]{0:T(128)} %param.9) | copy-start | bytes 52
  1.9 5.2 %collective-permute-start = (f32[7,4,16,3]{3,2,1,0:T(8,128)S(1)}, f32[7,4,16,3]{3,2,1,0:T(8,128)S(1)}, u32[]{:S(2)}, u32[]{:S(2)}) collective-permute-start(f32[7,4,16,3]{3,2,1,0:T(8,128)S(1)} %get-tuple-element.89), channel_id=1, source_target_pairs={{0,1},{1,2},{2,3},{3,4},{4,5},{5,6},{6,7},{7,8},{8,9},{9,10},{10,1... | collective-permute-start | bytes 16136 | tf_op jit(solution)/shard_map/ppermute | solution.py:19
  4.2 5.4 %collective-permute-start.1 = (f32[7,4,16,3]{3,2,1,0:T(8,128)S(1)}, f32[7,4,16,3]{3,2,1,0:T(8,128)S(1)}, u32[]{:S(2)}, u32[]{:S(2)}) collective-permute-start(f32[7,4,16,3]{3,2,1,0:T(8,128)S(1)} %get-tuple-element.90), channel_id=1, source_target_pairs={{1,0},{2,1},{3,2},{4,3},{5,4},{6,5},{7,6},{8,7},{9,8},{10,9},{11,1... | collective-permute-start | bytes 16136 | tf_op jit(solution)/shard_map/ppermute | solution.py:22
  11.8 0.7 copy-start.4
  12.5 5.5 %collective-permute-start.2 = (f32[7,4,16,256]{3,2,1,0:T(8,128)S(1)}, f32[7,4,16,256]{3,2,1,0:T(8,128)S(1)}, u32[]{:S(2)}, u32[]{:S(2)}) collective-permute-start(f32[7,4,16,256]{3,2,1,0:T(8,128)S(1)} %fusion.4), channel_id=1, source_target_pairs={{31,0},{0,1},{1,2},{2,3},{3,4},{4,5},{5,6},{6,7},{7,8},{8,9},{9,10... | collective-permute-start | bytes 1376264 | tf_op jit(solution)/shard_map/ppermute | solution.py:30
  18.1 13.5 %collective-permute-start.3 = (f32[7,4,16,256]{3,2,1,0:T(8,128)S(1)}, f32[7,4,16,256]{3,2,1,0:T(8,128)S(1)}, u32[]{:S(2)}, u32[]{:S(2)}) collective-permute-start(f32[7,4,16,256]{3,2,1,0:T(8,128)S(1)} %broadcast_select_fusion), channel_id=1, source_target_pairs={{30,0},{31,1},{0,2},{1,3},{2,4},{3,5},{4,6},{5,7},{6,8},{7,9},{8,1... | collective-permute-start | bytes 1376264 | tf_op jit(solution)/shard_map/ppermute | solution.py:30
  31.7 12.6 %collective-permute-start.4 = (f32[7,4,16,256]{3,2,1,0:T(8,128)S(1)}, f32[7,4,16,256]{3,2,1,0:T(8,128)S(1)}, u32[]{:S(2)}, u32[]{:S(2)}) collective-permute-start(f32[7,4,16,256]{3,2,1,0:T(8,128)S(1)} %broadcast_select_fusion.1), channel_id=1, source_target_pairs={{28,0},{29,1},{30,2},{31,3},{0,4},{1,5},{2,6},{3,7},{4,8},{5,9},{6... | collective-permute-start | bytes 1376264 | tf_op jit(solution)/shard_map/ppermute | solution.py:30
  44.5 23.3 %collective-permute-start.5 = (f32[7,4,16,256]{3,2,1,0:T(8,128)S(1)}, f32[7,4,16,256]{3,2,1,0:T(8,128)S(1)}, u32[]{:S(2)}, u32[]{:S(2)}) collective-permute-start(f32[7,4,16,256]{3,2,1,0:T(8,128)S(1)} %broadcast_select_fusion.2), channel_id=1, source_target_pairs={{24,0},{25,1},{26,2},{27,3},{28,4},{29,5},{30,6},{31,7},{0,8},{1,9... | collective-permute-start | bytes 1376264 | tf_op jit(solution)/shard_map/ppermute | solution.py:30
  68.0 10.4 %collective-permute-start.6 = (f32[7,4,16,256]{3,2,1,0:T(8,128)S(1)}, f32[7,4,16,256]{3,2,1,0:T(8,128)S(1)}, u32[]{:S(2)}, u32[]{:S(2)}) collective-permute-start(f32[7,4,16,256]{3,2,1,0:T(8,128)S(1)} %broadcast_select_fusion.3), channel_id=1, source_target_pairs={{16,0},{17,1},{18,2},{19,3},{20,4},{21,5},{22,6},{23,7},{24,8},{25... | collective-permute-start | bytes 1376264 | tf_op jit(solution)/shard_map/ppermute | solution.py:30
  78.5 33.2 %collective-permute-start.7 = (f32[7,4,16,256]{3,2,1,0:T(8,128)S(1)}, f32[7,4,16,256]{3,2,1,0:T(8,128)S(1)}, u32[]{:S(2)}, u32[]{:S(2)}) collective-permute-start(f32[7,4,16,256]{3,2,1,0:T(8,128)S(1)} %broadcast_select_fusion.4), channel_id=1, source_target_pairs={{31,0},{0,1},{1,2},{2,3},{3,4},{4,5},{5,6},{6,7},{7,8},{8,9},{9,10... | collective-permute-start | bytes 1376264 | tf_op jit(solution)/shard_map/ppermute | solution.py:30
  132.4 8.2 %collective-permute-start.9 = (f32[7,2,16,256]{3,2,1,0:T(8,128)S(1)}, f32[7,2,16,256]{3,2,1,0:T(8,128)S(1)}, u32[]{:S(2)}, u32[]{:S(2)}) collective-permute-start(f32[7,2,16,256]{3,2,1,0:T(8,128)S(1)} %copy.870), channel_id=1, source_target_pairs={{32,0},{64,32},{96,64},{128,96},{160,128},{192,160},{224,192},{0,2... | collective-permute-start | bytes 688136 | tf_op jit(solution)/shard_map/ppermute | solution.py:22
  137.6 8.5 %collective-permute-start.8 = (f32[7,2,16,256]{3,2,1,0:T(8,128)S(1)}, f32[7,2,16,256]{3,2,1,0:T(8,128)S(1)}, u32[]{:S(2)}, u32[]{:S(2)}) collective-permute-start(f32[7,2,16,256]{3,2,1,0:T(8,128)S(1)} %copy.869), channel_id=1, source_target_pairs={{0,32},{32,64},{64,96},{96,128},{128,160},{160,192},{192,224},{224... | collective-permute-start | bytes 688136 | tf_op jit(solution)/shard_map/ppermute | solution.py:19
  146.4 9.4 %collective-permute-start.10 = (f32[7,8,16,2]{3,2,1,0:T(8,128)S(1)}, f32[7,8,16,2]{3,2,1,0:T(8,128)S(1)}, u32[]{:S(2)}, u32[]{:S(2)}) collective-permute-start(f32[7,8,16,2]{3,2,1,0:T(8,128)S(1)} %get-tuple-element.85), channel_id=1, source_target_pairs={{0,1},{1,2},{2,3},{3,4},{4,5},{5,6},{6,7},{7,8},{8,9},{9,10},{10,1... | collective-permute-start | bytes 21512 | tf_op jit(solution)/shard_map/ppermute | solution.py:19
  150.4 7.9 %collective-permute-start.11 = (f32[7,8,16,2]{3,2,1,0:T(8,128)S(1)}, f32[7,8,16,2]{3,2,1,0:T(8,128)S(1)}, u32[]{:S(2)}, u32[]{:S(2)}) collective-permute-start(f32[7,8,16,2]{3,2,1,0:T(8,128)S(1)} %get-tuple-element.86), channel_id=1, source_target_pairs={{1,0},{2,1},{3,2},{4,3},{5,4},{6,5},{7,6},{8,7},{9,8},{10,9},{11,1... | collective-permute-start | bytes 21512 | tf_op jit(solution)/shard_map/ppermute | solution.py:22
where the time goes:
time: 174 us
  waiting for transfers between devices  84.8 us (49%)
  starting transfers between devices  44.3 us (25%)
  local copies, waits for them, and re-layouts  27.1 us (16%)
  other arithmetic  16.6 us (10%)
    ppermute x6, waiting for transfers between devices, passed_along(): return lax.ppermute(block, axis, route)  65.7 us
    ppermute x6, starting transfers between devices, passed_along(): return lax.ppermute(block, axis, route)  32.8 us
    ppermute x3, waiting for transfers between devices, with_halo(): lax.ppermute(lax.slice_in_dim(block, block.shape[dim] - width, None, axis...  13.9 us
    concatenate x1, local copies, waits for them, and re-layouts, body(): joined = jnp.concatenate([lower_block, current], 3)  7.53 us
    gather x1, local copies, waits for them, and re-layouts, column_slice(): return lax.dynamic_slice_in_dim(piece, start, block_cells, 2)  6.57 us
    ppermute x3, starting transfers between devices, with_halo(): lax.ppermute(lax.slice_in_dim(block, block.shape[dim] - width, None, axis...  6.26 us
    slice x4, local copies, waits for them, and re-layouts, with_halo(): lax.slice_in_dim(block, block.shape[dim] - width, None, axis=dim)  6.2 us
    ppermute x3, starting transfers between devices, with_halo(): lax.ppermute(lax.slice_in_dim(block, 0, width, axis=dim), axis, backward)  5.23 us
  transfers between devices with their start and end apart: 12, of which 12 were waited for; matrix products, arithmetic and copies ran while one was open for 2% of the time, Pallas kernels for 0%

commit v1 on v0

v1 whole, which is shorter than its diff:
```python
import functools

import jax
import jax.numpy as jnp
from jax import lax
from jax.experimental import pallas as pl
from jax.experimental.pallas import tpu as pltpu
from jax.sharding import PartitionSpec as P

MESH = pl.DeviceIdType.MESH
TIME_STEP = 0.025
SOUND_SQUARED = 1.0
ORBIT_FREQ = 1.0
SHEAR_RATE = 1.5

ROWS = 8
PHI = 32
NZ = 16
LANES = 128
FIELDS = 7
TILE = 16
RING = PHI * TILE
CHUNKS = 2 * PHI
COLUMNS = ((0, 3), (1, 2))
GROUP = 8


def ring_exit(q, fraction, lane):
    def upward(values, by):
        turned = pltpu.roll(values, LANES - by, 2)
        return jnp.where(lane >= LANES - by, turned[1:], turned[:-1])

    def downward(values):
        turned = pltpu.roll(values, 1, 2)
        return jnp.where(lane == 0, turned[:-1], turned[1:])

    here = q[1:-1]
    one = upward(q, 1)[1:]
    two = upward(q, 2)[1:]
    before = downward(q)[:-1]
    face = 7.0 / 12.0 * (here + one) - 1.0 / 12.0 * (before + two)
    face = jnp.clip(face, jnp.minimum(here, one), jnp.maximum(here, one))
    left = jnp.concatenate([pltpu.roll(face[:1], 1, 2), downward(face)], 0)
    curvature = 6.0 * (here - 0.5 * (face + left))
    outgoing = fraction * (
        face - 0.5 * fraction * (face - left - (1.0 - 2.0 / 3.0 * fraction) * curvature)
    )
    return here[1:] - outgoing[1:] + downward(outgoing)


def transport_kernel(
    shift_ref, frac_ref, dens_ref, mom_ref, fld_ref, own_ref, halo_ref, five_ref,
    send_f, recv_f, send_b, turned, five, sem_fs, sem_fr, sem_bs, sem_br, sem_xs, sem_xr,
):
    row = lax.axis_index("row")
    me = lax.axis_index("phi")
    above = (lax.rem(row + 1, ROWS), me)
    below = (lax.rem(row + ROWS - 1, ROWS), me)
    barrier = pltpu.get_barrier_semaphore()

    def greet(t, carry):
        pl.semaphore_signal(
            barrier, inc=1, device_id=(row, lax.rem(me + t, PHI)), device_id_type=MESH
        )
        return carry

    lax.fori_loop(1, PHI, greet, 0)
    pl.semaphore_signal(barrier, inc=1, device_id=above, device_id_type=MESH)
    pl.semaphore_signal(barrier, inc=1, device_id=below, device_id_type=MESH)

    def source(f, x, zs, ys):
        if f == 0:
            return dens_ref[x, zs, ys]
        if f < 4:
            return mom_ref[f - 1, x, zs, ys]
        return fld_ref[f - 4, x, zs, ys]

    def arrange(stage):
        for side in range(2):
            for half in range(2):
                for zt in range(2):
                    for f in range(8):
                        first = (side * NZ + 8 * zt) * TILE + half * 8 + f
                        if f < FIELDS:
                            block = source(
                                f, COLUMNS[stage][side], slice(8 * zt, 8 * zt + 8),
                                slice(LANES * half, LANES * half + LANES),
                            )
                        else:
                            block = jnp.zeros((8, LANES), jnp.float32)
                        send_f[stage, pl.ds(first, 8, stride=TILE), :] = block

    def rows_of(index):
        return pl.ds(pl.multiple_of(index * TILE, TILE), TILE)

    def spread(stage, src, dst, send_sem, recv_sem):
        def one(t, carry):
            to = lax.rem(me + t, PHI)
            pltpu.make_async_remote_copy(
                src_ref=src.at[stage, rows_of(to), :],
                dst_ref=dst.at[stage, rows_of(me), :],
                send_sem=send_sem.at[stage],
                recv_sem=recv_sem.at[stage],
                device_id=(row, to),
                device_id_type=MESH,
            ).start()
            return carry

        lax.fori_loop(1, PHI, one, 0)

    def settle(stage, buffer, sem):
        part = buffer.at[stage, pl.ds(0, RING - TILE), :]
        pltpu.make_async_copy(part, part, sem.at[stage]).wait()

    arrange(0)
    pl.semaphore_wait(barrier, PHI - 1 + 2)
    spread(0, send_f, recv_f, sem_fs, sem_fr)
    arrange(1)
    spread(1, send_f, recv_f, sem_fs, sem_fr)

    lane = lax.broadcasted_iota(jnp.int32, (1, 8, LANES), 2)
    sub = lax.broadcasted_iota(jnp.int32, (1, 8, LANES), 1)
    spot = lane - 3 * sub

    def turn(stage):
        column = jnp.where(me < NZ, COLUMNS[stage][0], COLUMNS[stage][1])
        cells = shift_ref[column]
        fraction = frac_ref[column]
        blocks = lax.shift_right_logical(cells, 7)
        inner = cells & (LANES - 1)
        recv_f[stage, rows_of(me), :] = send_f[stage, rows_of(me), :]

        def leave(i, carry):
            first = i * 2 * GROUP

            def chunk(c):
                at = lax.rem(c + CHUNKS, CHUNKS)
                return recv_f[stage, pl.ds(pl.multiple_of(at * 8, 8), 8), :].reshape(1, 8, LANES)

            body = recv_f[stage, pl.ds(pl.multiple_of(first * 8, 8), 16 * GROUP), :]
            q = jnp.concatenate(
                [chunk(first - 2), chunk(first - 1), body.reshape(2 * GROUP, 8, LANES),
                 chunk(first + 2 * GROUP)], 0
            )
            exited = ring_exit(q, fraction, lane)
            rolled = pltpu.roll(exited, inner, 2)
            turned[pl.ds(first + 2, 2 * GROUP)] = rolled
            turned[pl.ds(first + 66, 2 * GROUP)] = rolled
            return carry

        lax.fori_loop(0, PHI // GROUP, leave, 0)
        turned[0:2] = turned[64:66]
        turned[130] = turned[66]

        def place(i, carry):
            first = i * 2 * GROUP
            start = first + 64 - blocks
            window = jnp.stack([turned[start + j] for j in range(2 * GROUP + 3)])
            out = jnp.where(lane >= inner, window[1:], window[:-1])
            pairs = out.reshape(GROUP + 1, 2, 8, LANES)
            lower = pairs[:GROUP, 0]
            main = out[1:-1].reshape(GROUP, 2, 8, LANES)
            upper = pairs[1:, 1]
            ends = jnp.where(lane == 0, pltpu.roll(lower, 1, 2), pltpu.roll(upper, 1, 2))
            packed = jnp.where(spot == 0, ends[:, :, 0:1], 0.0)
            packed = jnp.where(spot == 1, ends[:, :, 1:2], packed)
            packed = jnp.where(spot == 2, ends[:, :, 2:3], packed)
            packed = jnp.sum(packed, axis=1, keepdims=True)
            low = jnp.where(sub == 7, packed, main[:, 0])
            both = jnp.concatenate([low[:, None], main[:, 1:]], 1)
            send_b[stage, pl.ds(pl.multiple_of(first * 8, 8), 16 * GROUP), :] = both.reshape(
                16 * GROUP, LANES
            )
            return carry

        lax.fori_loop(0, PHI // GROUP, place, 0)

    for stage in range(2):
        settle(stage, recv_f, sem_fr)
        turn(stage)
        spread(stage, send_b, own_ref, sem_bs, sem_br)
        own_ref[stage, rows_of(me), :] = send_b[stage, rows_of(me), :]

    half = NZ * TILE
    settle(0, own_ref, sem_br)
    upward = pltpu.make_async_remote_copy(
        src_ref=own_ref.at[0, pl.ds(half, half), :], dst_ref=halo_ref.at[0],
        send_sem=sem_xs.at[0], recv_sem=sem_xr.at[0], device_id=above, device_id_type=MESH,
    )
    downward = pltpu.make_async_remote_copy(
        src_ref=own_ref.at[0, pl.ds(0, half), :], dst_ref=halo_ref.at[1],
        send_sem=sem_xs.at[1], recv_sem=sem_xr.at[1], device_id=below, device_id_type=MESH,
    )
    upward.start()
    downward.start()
    settle(1, own_ref, sem_br)
    for k in range(2):
        ends = own_ref[1, pl.ds(8 * 2 * k + 7, 8, stride=2 * TILE), :]
        five[k, :, 0:LANES] = own_ref[1, pl.ds(16 * k + 4, 8, stride=2 * TILE), :]
        five[k, :, LANES:2 * LANES] = own_ref[1, pl.ds(16 * k + 12, 8, stride=2 * TILE), :]
        five[k, :, 2 * LANES:] = pltpu.roll(ends, LANES - 13, 1)
    second = pltpu.make_async_remote_copy(
        src_ref=five, dst_ref=five_ref,
        send_sem=sem_xs.at[2], recv_sem=sem_xr.at[2], device_id=below, device_id_type=MESH,
    )
    second.start()
    upward.wait()
    downward.wait()
    second.wait()
    for stage in range(2):
        settle(stage, send_f, sem_fs)
        settle(stage, send_b, sem_bs)


def up_z(values):
    return jnp.concatenate([values[1:2], pltpu.roll(values[0:1], 7, 1)], 0)


def low_z(values):
    return jnp.concatenate([pltpu.roll(values[1:2], 1, 1), values[0:1]], 0)


def up_y(values):
    return pltpu.roll(values, values.shape[2] - 1, 2)


def low_y(values):
    return pltpu.roll(values, 1, 2)


def same(values):
    return values


def cell_of(state, upper_bx):
    rho, mx, my, mz, bx, by, bz = state
    inv = 1.0 / rho
    m = (mx, my, mz)
    v = (mx * inv, my * inv, mz * inv)
    b = (0.5 * (bx + upper_bx), 0.5 * (by + up_y(by)), 0.5 * (bz + up_z(bz)))
    return dict(rho=rho, inv=inv, m=m, v=v, b=b, faces=(bx, by, bz))


def side_of(cell, n):
    t, u = [c for c in range(3) if c != n]
    m, v, b = cell["m"], cell["v"], cell["b"]
    across = b[t] * b[t] + b[u] * b[u]
    return dict(
        m=m, v=v, b=b, inv=cell["inv"], rho=cell["rho"],
        base=SOUND_SQUARED + across * cell["inv"],
        speed=jnp.abs(v[n]),
        push=m[n] * v[n] + (cell["rho"] * SOUND_SQUARED + 0.5 * across),
    )


def face_flux(low, high, normal, n, moved, wanted):
    others = [c for c in range(3) if c != n]
    square = normal * normal

    def fast(side, shifted):
        return shifted(side["speed"]) + jnp.sqrt(shifted(side["base"]) + square * shifted(side["inv"]))

    fastest = jnp.maximum(fast(low, moved), fast(high, same))
    result = {}

    def blend(flux_low, flux_high, state_low, state_high):
        return (flux_low + flux_high) - fastest * (state_high - state_low)

    if "mass" in wanted:
        result["mass"] = blend(moved(low["m"][n]), high["m"][n], moved(low["rho"]), high["rho"])
    if "m" in wanted:
        moms = [None] * 3
        moms[n] = blend(moved(low["push"]), high["push"], moved(low["m"][n]), high["m"][n]) - square
        for t in others:
            moms[t] = blend(
                moved(low["m"][t] * low["v"][n]), high["m"][t] * high["v"][n],
                moved(low["m"][t]), high["m"][t],
            ) - normal * (moved(low["b"][t]) + high["b"][t])
        result["m"] = moms
    for t in others:
        if ("b", t) in wanted:
            result["b", t] = blend(
                moved(low["b"][t] * low["v"][n]), high["b"][t] * high["v"][n],
                moved(low["b"][t]), high["b"][t],
            ) - normal * (moved(low["v"][t]) + high["v"][t])
    return result


def godunov(load, five, store):
    states = {i: load(i) for i in range(-1, 5)}
    cells = {}
    for i in range(-1, 5):
        cells[i] = cell_of(states[i], states[i + 1][4] if i < 4 else five)
    xs = {}
    for i in range(0, 5):
        if i == 0:
            low = side_of(cells[-1], 0)
        high = side_of(cells[i], 0)
        xs[i] = face_flux(low, high, cells[i]["faces"][0], 0, same, ("mass", "m", ("b", 1), ("b", 2)))
        low = high
    ys, zs = {}, {}
    for i in range(-1, 5):
        inner = 0 <= i < 4
        side = side_of(cells[i], 1)
        ys[i] = face_flux(
            side, side, cells[i]["faces"][1], 1, low_y,
            ("mass", "m", ("b", 0), ("b", 2)) if inner else (("b", 0),),
        )
        side = side_of(cells[i], 2)
        zs[i] = face_flux(
            side, side, cells[i]["faces"][2], 2, low_z,
            ("mass", "m", ("b", 0), ("b", 1)) if inner else (("b", 0),),
        )
    edge_z, edge_y, edge_x = {}, {}, {}
    for i in range(0, 5):
        edge_z[i] = ys[i]["b", 0] + ys[i - 1]["b", 0] - (xs[i]["b", 1] + low_y(xs[i]["b", 1]))
        edge_y[i] = xs[i]["b", 2] + low_z(xs[i]["b", 2]) - (zs[i]["b", 0] + zs[i - 1]["b", 0])
        if i < 4:
            edge_x[i] = zs[i]["b", 1] + low_y(zs[i]["b", 1]) - (ys[i]["b", 2] + low_z(ys[i]["b", 2]))
    step = 0.5 * TIME_STEP
    edge_step = 0.125 * TIME_STEP
    for i in range(0, 4):
        cell = cells[i]

        def divergence(pick):
            y, z = pick(ys[i]), pick(zs[i])
            return (pick(xs[i + 1]) - pick(xs[i])) + (up_y(y) - y) + (up_z(z) - z)

        store(0, i, cell["rho"] - step * divergence(lambda flux: flux["mass"]))
        new = [cell["m"][c] - step * divergence(lambda flux: flux["m"][c]) for c in range(3)]
        new[0] = new[0] + TIME_STEP * 2.0 * ORBIT_FREQ * cell["m"][1]
        new[1] = new[1] - TIME_STEP * (2.0 - SHEAR_RATE) * ORBIT_FREQ * cell["m"][0]
        for c in range(3):
            store(1 + c, i, new[c])
        bx, by, bz = cell["faces"]
        ez, ey, ex = edge_z[i], edge_y[i], edge_x[i]
        store(4, i, bx - edge_step * ((up_y(ez) - ez) - (up_z(ey) - ey)))
        store(5, i, by - edge_step * ((up_z(ex) - ex) - (edge_z[i + 1] - ez)))
        store(6, i, bz - edge_step * ((edge_y[i + 1] - ey) - (up_y(ex) - ex)))


def update_kernel(own_ref, halo_ref, five_ref, dens_ref, mom_ref, fld_ref, weave):
    def load(i):
        if i == -1:
            part, base = halo_ref.at[0], 0
        elif i == 4:
            part, base = halo_ref.at[1], 0
        else:
            part = own_ref.at[0 if i in (0, 3) else 1]
            base = 0 if i < 2 else NZ * TILE
        result = []
        for f in range(FIELDS):
            pieces = []
            for k in range(2):
                first = base + k * TILE
                ends = part[pl.ds(first + 7, 8, stride=2 * TILE), :]
                pieces.append(jnp.concatenate([
                    part[pl.ds(first + f, 8, stride=2 * TILE), :],
                    part[pl.ds(first + 8 + f, 8, stride=2 * TILE), :],
                    pltpu.roll(ends, LANES - (3 * f + 1), 1),
                ], 1)[None])
            result.append(jnp.concatenate(pieces, 0))
        return result

    def store(f, i, values):
        for half in range(2):
            for k in range(2):
                weave[f, i, half, pl.ds(k, 8, stride=2), :] = values[k, :, half * LANES:half * LANES + LANES]
            block = weave[f, i, half]
            ys = slice(half * LANES, half * LANES + LANES)
            if f == 0:
                dens_ref[i, :, ys] = block
            elif f < 4:
                mom_ref[f - 1, i, :, ys] = block
            else:
                fld_ref[f - 4, i, :, ys] = block

    godunov(load, five_ref[...], store)


def body(density, momentum, field, shift, frac):
    vmem = pl.BlockSpec(memory_space=pltpu.VMEM)
    smem = pl.BlockSpec(memory_space=pltpu.SMEM)
    f32 = jnp.float32
    own, halo, five = pl.pallas_call(
        transport_kernel,
        out_shape=(
            jax.ShapeDtypeStruct((2, RING, LANES), f32),
            jax.ShapeDtypeStruct((2, NZ * TILE, LANES), f32),
            jax.ShapeDtypeStruct((2, 8, 3 * LANES), f32),
        ),
        in_specs=[smem, smem, vmem, vmem, vmem],
        out_specs=(vmem, vmem, vmem),
        scratch_shapes=[
            pltpu.VMEM((2, RING, LANES), f32),
            pltpu.VMEM((2, RING, LANES), f32),
            pltpu.VMEM((2, RING, LANES), f32),
            pltpu.VMEM((131, 8, LANES), f32),
            pltpu.VMEM((2, 8, 3 * LANES), f32),
            pltpu.SemaphoreType.DMA((2,)),
            pltpu.SemaphoreType.DMA((2,)),
            pltpu.SemaphoreType.DMA((2,)),
            pltpu.SemaphoreType.DMA((2,)),
            pltpu.SemaphoreType.DMA((3,)),
            pltpu.SemaphoreType.DMA((3,)),
        ],
        compiler_params=pltpu.CompilerParams(
            collective_id=0, has_side_effects=True, vmem_limit_bytes=32 * 2**20
        ),
        name="transport",
    )(shift, frac, density, momentum, field)
    return pl.pallas_call(
        update_kernel,
        out_shape=(
            jax.ShapeDtypeStruct(density.shape, f32),
            jax.ShapeDtypeStruct(momentum.shape, f32),
            jax.ShapeDtypeStruct(field.shape, f32),
        ),
        in_specs=[vmem, vmem, vmem],
        out_specs=(vmem, vmem, vmem),
        scratch_shapes=[pltpu.VMEM((FIELDS, 4, 2, NZ, LANES), f32)],
        compiler_params=pltpu.CompilerParams(vmem_limit_bytes=32 * 2**20),
        name="update",
    )(own, halo, five)


def solution(mesh):
    return jax.shard_map(
        body,
        mesh=mesh,
        in_specs=(
            P("row", None, "phi"),
            P(None, "row", None, "phi"),
            P(None, "row", None, "phi"),
            P("row"),
            P("row"),
        ),
        out_specs=(P("row", None, "phi"), P(None, "row", None, "phi"), P(None, "row", None, "phi")),
        check_vma=False,
    )
```

time: 174 us -> 49 us (0.28)
  the two profiles are of different devices: /device:TPU:65 before, /device:TPU:1 now
where the time goes in v1:
time: 49 us; the launch traced here: 48.8 us
  Pallas kernels  44.1 us (90%)
  local copies, waits for them, and re-layouts  3.99 us (8%)
  between operations  0.65 us (1%)
    pallas_call x1, Pallas kernels, body(): pl.pallas_call(transport_kernel, out_shape=(jax.ShapeDtypeStruct((2, RING...  41.8 us
    unnamed x10, local copies, waits for them, and re-layouts  3.99 us
    pallas_call x1, Pallas kernels, body(): pl.pallas_call(update_kernel, out_shape=(jax.ShapeDtypeStruct(density.sha...  2.37 us

profile of v1, /device:TPU:1, one launch (start us, length us, event | category | flops | bytes accessed | tf_op | source)
XLA Modules:
  0.0 48.8 jit_solution(15970635025102549643)
XLA Ops:
  0.6 0.0 copy-start
  0.6 0.9 %copy-done = f32[3,4,16,256]{3,2,1,0:T(8,128)S(1)} copy-done((f32[3,4,16,256]{3,2,1,0:T(8,128)S(1)}, f32[3,4,16,256]{3,2,1,0:T(8,128)}, u32[]{:S(2)}) %copy-start) | copy-done | bytes 196632
  1.6 0.0 copy-start.1
  1.6 0.9 %copy-done.1 = f32[3,4,16,256]{3,2,1,0:T(8,128)S(1)} copy-done((f32[3,4,16,256]{3,2,1,0:T(8,128)S(1)}, f32[3,4,16,256]{3,2,1,0:T(8,128)}, u32[]{:S(2)}) %copy-start.1) | copy-done | bytes 196632
  2.5 0.0 copy-start.2
  2.5 0.8 %copy-done.2 = f32[4,16,256]{2,1,0:T(8,128)S(1)} copy-done((f32[4,16,256]{2,1,0:T(8,128)S(1)}, f32[4,16,256]{2,1,0:T(8,128)}, u32[]{:S(2)}) %copy-start.2) | copy-done | bytes 65560
  3.3 0.0 copy-start.3
  3.3 0.7 %copy-done.3 = s32[4]{0:T(128)S(1)} copy-done((s32[4]{0:T(128)S(1)}, s32[4]{0:T(128)}, u32[]{:S(2)}) %copy-start.3) | copy-done | bytes 40
  4.0 0.0 copy-start.4
  4.0 0.7 %copy-done.4 = f32[4]{0:T(128)S(1)} copy-done((f32[4]{0:T(128)S(1)}, f32[4]{0:T(128)}, u32[]{:S(2)}) %copy-start.4) | copy-done | bytes 40
  4.6 41.8 %transport.1 = (f32[2,512,128]{2,1,0:T(8,128)S(1)}, f32[2,256,128]{2,1,0:T(8,128)S(1)}, f32[2,8,384]{2,1,0:T(8,128)S(1)}) custom-call(s32[4]{0:T(128)S(1)} %copy-done.3, f32[4]{0:T(128)S(1)} %copy-done.4, f32[4,16,256]{2,1,0:T(8,128)S(1)} %copy-done.2, f32[3,4,16,256]{3,2,1,0:T(8,128)S(1)} %copy-done, f32[3,4,16,256]{3,2,1,0:T(8,128)S(1)} %copy-done.1), custom_call_target="tpu_custom_call" | custom-call | tf_op jit(solution)/shard_map/transport/pallas_call | solution.py:385
  46.4 2.4 %update.1 = (f32[4,16,256]{2,1,0:T(8,128)}, f32[3,4,16,256]{3,2,1,0:T(8,128)}, f32[3,4,16,256]{3,2,1,0:T(8,128)}) custom-call(f32[2,512,128]{2,1,0:T(8,128)S(1)} %get-tuple-element.6.own_ref, f32[2,256,128]{2,1,0:T(8,128)S(1)} %get-tuple-element.7.halo_ref, f32[2,8,384]{2,1,0:T(8,128)S(1)} %get-tuple-element.8.five_ref), custom_call_target="tpu_custom_call" | custom-call | tf_op jit(solution)/shard_map/update/pallas_call | solution.py:412
Async XLA Ops:
  0.6 0.9 %copy-start = (f32[3,4,16,256]{3,2,1,0:T(8,128)S(1)}, f32[3,4,16,256]{3,2,1,0:T(8,128)}, u32[]{:S(2)}) copy-start(f32[3,4,16,256]{3,2,1,0:T(8,128)} %mom_ref.1) | copy-start | bytes 589828
  1.6 0.9 %copy-start.1 = (f32[3,4,16,256]{3,2,1,0:T(8,128)S(1)}, f32[3,4,16,256]{3,2,1,0:T(8,128)}, u32[]{:S(2)}) copy-start(f32[3,4,16,256]{3,2,1,0:T(8,128)} %fld_ref.1) | copy-start | bytes 589828
  2.5 0.8 %copy-start.2 = (f32[4,16,256]{2,1,0:T(8,128)S(1)}, f32[4,16,256]{2,1,0:T(8,128)}, u32[]{:S(2)}) copy-start(f32[4,16,256]{2,1,0:T(8,128)} %dens_ref.1) | copy-start | bytes 196612
  3.3 0.7 %copy-start.3 = (s32[4]{0:T(128)S(1)}, s32[4]{0:T(128)}, u32[]{:S(2)}) copy-start(s32[4]{0:T(128)} %shift_ref.1) | copy-start | bytes 52
  4.0 0.7 %copy-start.4 = (f32[4]{0:T(128)S(1)}, f32[4]{0:T(128)}, u32[]{:S(2)}) copy-start(f32[4]{0:T(128)} %frac_ref.1) | copy-start | bytes 52

commit v2 on v0

v2 whole, which is shorter than its diff:
```python
import functools

import jax
import jax.numpy as jnp
from jax import lax
from jax.experimental import pallas as pl
from jax.experimental.pallas import tpu as pltpu
from jax.sharding import PartitionSpec as P

MESH = pl.DeviceIdType.MESH
TIME_STEP = 0.025
SOUND_SQUARED = 1.0
ORBIT_FREQ = 1.0
SHEAR_RATE = 1.5

ROWS = 8
PHI = 32
NZ = 16
LANES = 128
FIELDS = 7
PARTS = 4
COLUMNS = ((0, 3), (0, 3), (1, 2), (1, 2))
FIRST = (0, 4, 0, 4)
TILE = 8
RING = PHI * TILE
HALF = RING // 2
OUT_ROWS = (8, 8, 8, 6)
UPPER = (4, 4, 4, 3)
BACK_ROWS = (8, 8, 8, 7)


def after(values, by):
    return jnp.concatenate([values[by:], values[:by]], 0)


def ring_exit(q, fraction, lane, later, earlier):
    def upward(by):
        turned = pltpu.roll(q, LANES - by, 2)
        return jnp.where(lane >= LANES - by, later(turned), turned)

    def downward(values):
        turned = pltpu.roll(values, 1, 2)
        return jnp.where(lane == 0, earlier(turned), turned)

    one, two, before = upward(1), upward(2), downward(q)
    face = 7.0 / 12.0 * (q + one) - 1.0 / 12.0 * (before + two)
    face = jnp.clip(face, jnp.minimum(q, one), jnp.maximum(q, one))
    left = downward(face)
    curvature = 6.0 * (q - 0.5 * (face + left))
    outgoing = fraction * (
        face - 0.5 * fraction * (face - left - (1.0 - 2.0 / 3.0 * fraction) * curvature)
    )
    return q - outgoing + downward(outgoing)


def step_kernel(
    shift_hbm, frac_hbm, dens_hbm, mom_hbm, fld_hbm, dens_out, mom_out, fld_out,
    shift_ref, frac_ref, dens_ref, mom_ref, fld_ref, send_f, recv_f, send_b, turned, tails, own_ref, halo_ref,
    five, five_ref, weave, sem_in, sem_fs, sem_fr, sem_bs, sem_br, sem_xs, sem_xr, sem_out,
):
    row = lax.axis_index("row")
    me = lax.axis_index("phi")
    above = (lax.rem(row + 1, ROWS), me)
    below = (lax.rem(row + ROWS - 1, ROWS), me)
    barrier = pltpu.get_barrier_semaphore()

    def greet(t, carry):
        pl.semaphore_signal(
            barrier, inc=1, device_id=(row, lax.rem(me + t, PHI)), device_id_type=MESH
        )
        return carry

    lax.fori_loop(1, PHI, greet, 0)
    pl.semaphore_signal(barrier, inc=1, device_id=above, device_id_type=MESH)
    pl.semaphore_signal(barrier, inc=1, device_id=below, device_id_type=MESH)

    fetches = [
        pltpu.make_async_copy(src, dst, sem_in.at[k])
        for k, (src, dst) in enumerate((
            (dens_hbm, dens_ref), (mom_hbm, mom_ref), (fld_hbm, fld_ref),
            (shift_hbm, shift_ref), (frac_hbm, frac_ref),
        ))
    ]
    for fetch in fetches:
        fetch.start()

    def source(f, x, zs, ys):
        if f == 0:
            return dens_ref[x, zs, ys]
        if f < 4:
            return mom_ref[f - 1, x, zs, ys]
        return fld_ref[f - 4, x, zs, ys]

    def arrange(part):
        for side in range(2):
            for half in range(2):
                for zt in range(2):
                    for j in range(3 if part == 3 else 4):
                        f, x = FIRST[part] + j, COLUMNS[part][side]
                        if f == FIELDS:
                            f, x = 4, 1
                        block = source(
                            f, x, slice(8 * zt, 8 * zt + 8), slice(LANES * half, LANES * half + LANES)
                        )
                        first = (side * NZ + 8 * zt) * TILE + half * UPPER[part] + j
                        send_f[part, pl.ds(first, 8, stride=TILE), :] = block

    def rows_of(index, count=TILE):
        return pl.ds(pl.multiple_of(index * TILE, TILE), count)

    def spread(part, count, src, dst, send_sem, recv_sem):
        def one(t, carry):
            to = lax.rem(me + t, PHI)
            pltpu.make_async_remote_copy(
                src_ref=src.at[part, rows_of(to, count), :],
                dst_ref=dst.at[part, rows_of(me, count), :],
                send_sem=send_sem.at[part],
                recv_sem=recv_sem.at[part],
                device_id=(row, to),
                device_id_type=MESH,
            ).start()
            return carry

        lax.fori_loop(1, PHI, one, 0)

    def settle(part, count, buffer, sem):
        rows = buffer.at[part, pl.ds(0, (PHI - 1) * count), :]
        pltpu.make_async_copy(rows, rows, sem.at[part]).wait()

    def send_out(part):
        spread(part, OUT_ROWS[part], send_f, recv_f, sem_fs, sem_fr)

    lane = lax.broadcasted_iota(jnp.int32, (1, 8, LANES), 2)
    sub = lax.broadcasted_iota(jnp.int32, (1, 8, LANES), 1)
    lower = sub < 4
    spare = (sub & 3) == 3

    def later(values):
        return pltpu.roll(jnp.where(lower, after(values, 1), values), 4, 1)

    def earlier(values):
        return pltpu.roll(jnp.where(lower, values, after(values, -1)), 4, 1)

    def turn(part):
        settle(part, OUT_ROWS[part], recv_f, sem_fr)
        recv_f[part, rows_of(me), :] = send_f[part, rows_of(me), :]
        column = jnp.where(me < NZ, COLUMNS[part][0], COLUMNS[part][1])
        fraction = frac_ref[column]
        cells = shift_ref[column]
        inner = cells & (LANES - 1)
        if part == 1:
            fraction = jnp.where(spare, frac_ref[1], fraction)
            cells_1 = shift_ref[1]
            inner_1 = cells_1 & (LANES - 1)
        q = recv_f[part].reshape(PHI, 8, LANES)
        if part == 3:
            q = jnp.where(lower, q, pltpu.roll(q, 1, 1))
        exited = ring_exit(q, fraction, lane, later, earlier)
        rolled = pltpu.roll(exited, inner, 2)
        if part == 1:
            rolled = jnp.where(spare, pltpu.roll(exited, inner_1, 2), rolled)
        turned[0:PHI] = rolled
        turned[PHI:] = rolled

        def moved(amount):
            start = PHI - lax.shift_right_logical(amount, 8)
            blocks = jnp.stack([turned[start + j] for j in range(PHI)])
            return jnp.where((amount & LANES) == 0, blocks, earlier(blocks))

        out, split = moved(cells), inner
        if part == 1:
            out, split = jnp.where(spare, moved(cells_1), out), jnp.where(spare, inner_1, inner)
        out = jnp.where(lane >= split, out, earlier(out))
        ends = pltpu.roll(out, 1, 2)
        ends = jnp.where(lane == 0, pltpu.roll(after(ends, -1), 4, 1), after(ends, 1))
        spot = jnp.where(sub < (3 if part == 3 else 4), lane - 3 * (sub + FIRST[part]), -1)
        packed = jnp.where(spot == 0, ends[:, :, 0:1], 0.0)
        packed = jnp.where(spot == 1, ends[:, :, 1:2], packed)
        packed = jnp.where(spot == 2, ends[:, :, 2:3], packed)
        packed = jnp.sum(packed, axis=1, keepdims=True)
        if FIRST[part] == 0:
            tails[...] = jnp.broadcast_to(packed, tails.shape)
        else:
            packed = packed + tails[...]
            if part == 1:
                out = jnp.where((sub == 7) & (me < NZ), pltpu.roll(out, 4, 1), out)
            out = jnp.where(sub == 3, packed, out)
        send_b[part] = out.reshape(RING, LANES)
        spread(part, BACK_ROWS[part], send_b, own_ref, sem_bs, sem_br)
        own_ref[part, rows_of(me), :] = send_b[part, rows_of(me), :]

    def swap_of(k, src, dst, to):
        return pltpu.make_async_remote_copy(
            src_ref=src, dst_ref=dst, send_sem=sem_xs.at[k], recv_sem=sem_xr.at[k],
            device_id=to, device_id_type=MESH,
        )

    def swap(part):
        settle(part, BACK_ROWS[part], own_ref, sem_br)
        both = [
            swap_of(2 * part, own_ref.at[part, pl.ds(HALF, HALF), :], halo_ref.at[0, part], above),
            swap_of(2 * part + 1, own_ref.at[part, pl.ds(0, HALF), :], halo_ref.at[1, part], below),
        ]
        for each in both:
            each.start()
        return both

    for fetch in fetches:
        fetch.wait()
    arrange(0)
    pl.semaphore_wait(barrier, PHI - 1 + 2)
    send_out(0)
    arrange(1)
    send_out(1)
    arrange(2)
    send_out(2)
    arrange(3)
    turn(0)
    turn(1)
    send_out(3)
    turn(2)
    swaps = swap(0) + swap(1)
    for k in range(2):
        five[k] = own_ref[1, pl.ds(HALF + TILE * k + 7, 8, stride=2 * TILE), :]
    swaps.append(swap_of(4, five, five_ref, below))
    swaps[-1].start()
    turn(3)

    def gather(rows, ends, f):
        pieces = []
        for k in range(2):
            halves = [part[pl.ds(base + k * TILE + r, 8, stride=2 * TILE), :] for part, base, r in rows]
            part, base = ends
            tail = part[pl.ds(base + k * TILE + 3, 8, stride=2 * TILE), :]
            pieces.append(
                jnp.concatenate(halves + [pltpu.roll(tail, LANES - (3 * f + 1), 1)], 1)[None]
            )
        return jnp.concatenate(pieces, 0)

    def load(i):
        if i in (-1, 4):
            parts, base = [halo_ref.at[0 if i < 0 else 1, k] for k in range(2)], 0
        else:
            parts = [own_ref.at[(0 if i in (0, 3) else 2) + k] for k in range(2)]
            base = 0 if i < 2 else HALF
        return [
            gather([(parts[f // 4], base, f % 4), (parts[f // 4], base, 4 + f % 4)], (parts[1], base), f)
            for f in range(FIELDS)
        ]

    def load_one():
        part = own_ref.at[1]
        return gather([(part, 0, 7), (part, HALF, 7)], (part, 0), FIELDS)

    def load_five():
        part = halo_ref.at[1, 1]
        pieces = []
        for k in range(2):
            lower_half = part[pl.ds(k * TILE + 7, 8, stride=2 * TILE), :]
            tail = part[pl.ds(k * TILE + 3, 8, stride=2 * TILE), :]
            pieces.append(
                jnp.concatenate([lower_half, five_ref[k], pltpu.roll(tail, LANES - 22, 1)], 1)[None]
            )
        return jnp.concatenate(pieces, 0)

    step = Step(load, {1: load_one, 5: load_five})
    writes = []

    def finish(i, fields):
        for f in fields:
            values = step.result(f, i)
            for side in range(2):
                for k in range(2):
                    weave[f, i, side, pl.ds(k, 8, stride=2), :] = values[
                        k, :, side * LANES:side * LANES + LANES
                    ]
        for side in range(2):
            ys = pl.ds(side * LANES, LANES)
            for src, dst in (
                (weave.at[0, i, side], dens_out.at[i, :, ys]),
                (weave.at[pl.ds(1, 3), i, side], mom_out.at[:, i, :, ys]),
                (weave.at[pl.ds(4, 3), i, side], fld_out.at[:, i, :, ys]),
            ):
                write = pltpu.make_async_copy(src, dst, sem_out.at[len(writes)])
                write.start()
                writes.append(write)

    for each in swaps:
        each.wait()
    step.flux(0, 0)
    step.flux(4, 0)
    for i in (-1, 0, 3, 4):
        step.flux(i, 1)
        step.flux(i, 2)
    settle(2, BACK_ROWS[2], own_ref, sem_br)
    settle(3, BACK_ROWS[3], own_ref, sem_br)
    for i in range(4):
        finish(i, range(FIELDS))
    for part in range(PARTS):
        settle(part, OUT_ROWS[part], send_f, sem_fs)
        settle(part, BACK_ROWS[part], send_b, sem_bs)
    for write in writes:
        write.wait()


def up_z(values):
    return jnp.concatenate([values[1:2], pltpu.roll(values[0:1], 7, 1)], 0)


def low_z(values):
    return jnp.concatenate([pltpu.roll(values[1:2], 1, 1), values[0:1]], 0)


def up_y(values):
    return pltpu.roll(values, values.shape[2] - 1, 2)


def low_y(values):
    return pltpu.roll(values, 1, 2)


def same(values):
    return values


def face_flux(low, high, normal, n, moved, wanted):
    square = normal * normal

    def fast(side, shifted):
        return shifted(side["speed"]) + jnp.sqrt(shifted(side["base"]) + square * shifted(side["inv"]))

    fastest = jnp.maximum(fast(low, moved), fast(high, same))

    def blend(flux_low, flux_high, state_low, state_high):
        return (flux_low + flux_high) - fastest * (state_high - state_low)

    result = {}
    if "m" in wanted:
        result["m"] = [blend(moved(low["m"][n]), high["m"][n], moved(low["rho"]), high["rho"])]
        for t in range(3):
            if t == n:
                part = blend(moved(low["push"]), high["push"], moved(low["m"][n]), high["m"][n]) - square
            else:
                part = blend(
                    moved(low["m"][t] * low["v"][n]), high["m"][t] * high["v"][n],
                    moved(low["m"][t]), high["m"][t],
                ) - normal * (moved(low["b"][t]) + high["b"][t])
            result["m"].append(part)
    for t in range(3):
        if t in wanted:
            result[t] = blend(
                moved(low["b"][t] * low["v"][n]), high["b"][t] * high["v"][n],
                moved(low["b"][t]), high["b"][t],
            ) - normal * (moved(low["v"][t]) + high["v"][t])
    return result


class Step:
    def __init__(self, load, radial):
        self.load, self.radial, self.kept = load, radial, {}

    def keep(self, key, make):
        if key not in self.kept:
            self.kept[key] = make()
        return self.kept[key]

    def state(self, i):
        return self.keep(("state", i), lambda: self.load(i))

    def across(self, i, c):
        def make():
            faces = self.state(i)[4:]
            if c == 0:
                upper = self.radial[i + 1]() if i in (0, 4) else self.state(i + 1)[4]
            else:
                upper = up_y(faces[1]) if c == 1 else up_z(faces[2])
            return 0.5 * (faces[c] + upper)

        return self.keep(("across", i, c), make)

    def cell(self, i):
        def make():
            rho, mx, my, mz = self.state(i)[:4]
            inv = 1.0 / rho
            return dict(rho=rho, inv=inv, m=(mx, my, mz), v=(mx * inv, my * inv, mz * inv))

        return self.keep(("cell", i), make)

    def side(self, i, n):
        def make():
            cell = self.cell(i)
            t, u = [c for c in range(3) if c != n]
            b = {t: self.across(i, t), u: self.across(i, u)}
            square = b[t] * b[t] + b[u] * b[u]
            return dict(
                cell, b=b, base=SOUND_SQUARED + square * cell["inv"], speed=jnp.abs(cell["v"][n]),
                push=cell["m"][n] * cell["v"][n] + (cell["rho"] * SOUND_SQUARED + 0.5 * square),
            )

        return self.keep(("side", i, n), make)

    def flux(self, i, n):
        def make():
            inner = 0 <= i < 4
            normal = self.state(i)[4 + n]
            high = self.side(i, n)
            if n == 0:
                return face_flux(self.side(i - 1, 0), high, normal, 0, same, ("m", 1, 2))
            other = 3 - n
            return face_flux(
                high, high, normal, n, low_y if n == 1 else low_z, ("m", 0, other) if inner else (0,)
            )

        return self.keep(("flux", i, n), make)

    def edge(self, i, c):
        def make():
            if c == 2:
                by = self.flux(i, 0)[1]
                return self.flux(i, 1)[0] + self.flux(i - 1, 1)[0] - (by + low_y(by))
            if c == 1:
                bz = self.flux(i, 0)[2]
                return bz + low_z(bz) - (self.flux(i, 2)[0] + self.flux(i - 1, 2)[0])
            by, bz = self.flux(i, 2)[1], self.flux(i, 1)[2]
            return by + low_y(by) - (bz + low_z(bz))

        return self.keep(("edge", i, c), make)

    def result(self, f, i):
        step, edge_step = 0.5 * TIME_STEP, 0.125 * TIME_STEP
        if f < 4:
            y, z = self.flux(i, 1)["m"][f], self.flux(i, 2)["m"][f]
            total = (self.flux(i + 1, 0)["m"][f] - self.flux(i, 0)["m"][f]) + (up_y(y) - y) + (up_z(z) - z)
            new = self.state(i)[f] - step * total
            if f == 1:
                new = new + TIME_STEP * 2.0 * ORBIT_FREQ * self.state(i)[2]
            if f == 2:
                new = new - TIME_STEP * (2.0 - SHEAR_RATE) * ORBIT_FREQ * self.state(i)[1]
            return new
        if f == 4:
            ez, ey = self.edge(i, 2), self.edge(i, 1)
            curl = (up_y(ez) - ez) - (up_z(ey) - ey)
        elif f == 5:
            ex = self.edge(i, 0)
            curl = (up_z(ex) - ex) - (self.edge(i + 1, 2) - self.edge(i, 2))
        else:
            ex = self.edge(i, 0)
            curl = (self.edge(i + 1, 1) - self.edge(i, 1)) - (up_y(ex) - ex)
        return self.state(i)[f] - edge_step * curl


def pass_kernel(*refs):
    sources, targets, kept, sems = refs[:3], refs[3:6], refs[6:9], refs[9]
    inward = [pltpu.make_async_copy(src, dst, sems.at[0, k]) for k, (src, dst) in enumerate(zip(sources, kept))]
    outward = [pltpu.make_async_copy(src, dst, sems.at[1, k]) for k, (src, dst) in enumerate(zip(kept, targets))]
    for copy in inward:
        copy.start()
    for there, back in zip(inward, outward):
        there.wait()
        back.start()
    for copy in outward:
        copy.wait()


def body(density, momentum, field, shift, frac):
    hbm = pl.BlockSpec(memory_space=pl.ANY)
    f32 = jnp.float32
    shapes = tuple(jax.ShapeDtypeStruct(a.shape, f32) for a in (density, momentum, field))
    results = pl.pallas_call(
        step_kernel,
        out_shape=shapes,
        in_specs=[hbm] * 5,
        out_specs=(hbm,) * 3,
        scratch_shapes=[
            pltpu.SMEM(shift.shape, jnp.int32),
            pltpu.SMEM(frac.shape, f32),
            pltpu.VMEM(density.shape, f32),
            pltpu.VMEM(momentum.shape, f32),
            pltpu.VMEM(field.shape, f32),
            pltpu.VMEM((PARTS, RING, LANES), f32),
            pltpu.VMEM((PARTS, RING, LANES), f32),
            pltpu.VMEM((PARTS, RING, LANES), f32),
            pltpu.VMEM((2 * PHI, 8, LANES), f32),
            pltpu.VMEM((PHI, 8, LANES), f32),
            pltpu.VMEM((PARTS, RING, LANES), f32),
            pltpu.VMEM((2, 2, HALF, LANES), f32),
            pltpu.VMEM((2, 8, LANES), f32),
            pltpu.VMEM((2, 8, LANES), f32),
            pltpu.VMEM((FIELDS, 4, 2, NZ, LANES), f32),
            pltpu.SemaphoreType.DMA((5,)),
            pltpu.SemaphoreType.DMA((PARTS,)),
            pltpu.SemaphoreType.DMA((PARTS,)),
            pltpu.SemaphoreType.DMA((PARTS,)),
            pltpu.SemaphoreType.DMA((PARTS,)),
            pltpu.SemaphoreType.DMA((5,)),
            pltpu.SemaphoreType.DMA((5,)),
            pltpu.SemaphoreType.DMA((24,)),
        ],
        compiler_params=pltpu.CompilerParams(
            collective_id=0, has_side_effects=True, vmem_limit_bytes=56 * 2**20
        ),
        name="step",
    )(shift, frac, density, momentum, field)
    return pl.pallas_call(
        pass_kernel,
        out_shape=shapes,
        in_specs=[hbm] * 3,
        out_specs=(hbm,) * 3,
        scratch_shapes=[pltpu.VMEM(a.shape, f32) for a in shapes] + [pltpu.SemaphoreType.DMA((2, 3))],
        compiler_params=pltpu.CompilerParams(vmem_limit_bytes=56 * 2**20),
        name="hand_on",
    )(*results)


def solution(mesh):
    return jax.shard_map(
        body,
        mesh=mesh,
        in_specs=(
            P("row", None, "phi"),
            P(None, "row", None, "phi"),
            P(None, "row", None, "phi"),
            P("row"),
            P("row"),
        ),
        out_specs=(P("row", None, "phi"), P(None, "row", None, "phi"), P(None, "row", None, "phi")),
        check_vma=False,
    )
```

time: 174 us -> 42.8 us (0.25)
  the two profiles are of different devices: /device:TPU:65 before, /device:TPU:1 now
where the time goes in v2:
time: 42.8 us; the launch traced here: 42.7 us
  Pallas kernels  42.1 us (98%)
  between operations  0.64 us (1%)
    pallas_call x1, Pallas kernels, body(): pl.pallas_call(step_kernel, out_shape=shapes, in_specs=[hbm] * 5, out_spe...  40.3 us
    pallas_call x1, Pallas kernels, body(): pl.pallas_call(pass_kernel, out_shape=shapes, in_specs=[hbm] * 3, out_spe...  1.79 us

profile of v2, /device:TPU:1, one launch (start us, length us, event | category | flops | bytes accessed | tf_op | source)
XLA Modules:
  0.0 42.7 jit_solution(10499852219013339582)
XLA Ops:
  0.6 40.3 %step.1 = (f32[4,16,256]{2,1,0:T(8,128)}, f32[3,4,16,256]{3,2,1,0:T(8,128)}, f32[3,4,16,256]{3,2,1,0:T(8,128)}) custom-call(s32[4]{0:T(128)} %shift_hbm.1, f32[4]{0:T(128)} %frac_hbm.1, f32[4,16,256]{2,1,0:T(8,128)} %dens_hbm.1, f32[3,4,16,256]{3,2,1,0:T(8,128)} %mom_hbm.1, f32[3,4,16,256]{3,2,1,0:T(8,128)} %fld_hbm.1), custom_call_target="tpu_custom_call" | custom-call | tf_op jit(solution)/shard_map/step/pallas_call | solution.py:469
  40.9 1.8 %hand_on.1 = (f32[4,16,256]{2,1,0:T(8,128)}, f32[3,4,16,256]{3,2,1,0:T(8,128)}, f32[3,4,16,256]{3,2,1,0:T(8,128)}) custom-call(f32[4,16,256]{2,1,0:T(8,128)} %get-tuple-element.6.refs_0_, f32[3,4,16,256]{3,2,1,0:T(8,128)} %get-tuple-element.7.refs_1_, f32[3,4,16,256]{3,2,1,0:T(8,128)} %get-tuple-element.8.refs_2_), custom_call_target="tpu_custom_call" | custom-call | tf_op jit(solution)/shard_map/hand_on/pallas_call | solution.py:504

commit v3 on v2

--- a/solution.py
+++ b/solution.py
@@ -64,13 +64,20 @@
     below = (lax.rem(row + ROWS - 1, ROWS), me)
     barrier = pltpu.get_barrier_semaphore()
 
-    def greet(t, carry):
+    def partner(i):
+        k = i // 4
+        dz = 4 + (k + 1) // 2 * (1 - 2 * (k % 2))
+        z = lax.rem(me // 2 + dz + 8, 8)
+        x = lax.rem(me // 16 + 1 - i // 2 % 2, 2)
+        return x * 16 + z * 2 + lax.rem(me + 1 - i % 2, 2)
+
+    def greet(i, carry):
         pl.semaphore_signal(
-            barrier, inc=1, device_id=(row, lax.rem(me + t, PHI)), device_id_type=MESH
+            barrier, inc=1, device_id=(row, partner(i)), device_id_type=MESH
         )
         return carry
 
-    lax.fori_loop(1, PHI, greet, 0)
+    lax.fori_loop(0, PHI - 1, greet, 0)
     pl.semaphore_signal(barrier, inc=1, device_id=above, device_id_type=MESH)
     pl.semaphore_signal(barrier, inc=1, device_id=below, device_id_type=MESH)
 
@@ -109,8 +116,8 @@
         return pl.ds(pl.multiple_of(index * TILE, TILE), count)
 
     def spread(part, count, src, dst, send_sem, recv_sem):
-        def one(t, carry):
-            to = lax.rem(me + t, PHI)
+        def one(i, carry):
+            to = partner(i)
             pltpu.make_async_remote_copy(
                 src_ref=src.at[part, rows_of(to, count), :],
                 dst_ref=dst.at[part, rows_of(me, count), :],
@@ -121,7 +128,7 @@
             ).start()
             return carry
 
-        lax.fori_loop(1, PHI, one, 0)
+        lax.fori_loop(0, PHI - 1, one, 0)
 
     def settle(part, count, buffer, sem):
         rows = buffer.at[part, pl.ds(0, (PHI - 1) * count), :]
@@ -216,15 +223,16 @@
     send_out(2)
     arrange(3)
     turn(0)
+    send_out(3)
     turn(1)
-    send_out(3)
     turn(2)
-    swaps = swap(0) + swap(1)
+    swaps = swap(0)
+    turn(3)
+    swaps += swap(1)
     for k in range(2):
         five[k] = own_ref[1, pl.ds(HALF + TILE * k + 7, 8, stride=2 * TILE), :]
     swaps.append(swap_of(4, five, five_ref, below))
     swaps[-1].start()
-    turn(3)
 
     def gather(rows, ends, f):
         pieces = []
@@ -285,16 +293,20 @@
                 write.start()
                 writes.append(write)
 
+    step.flux(0, 1)
+    step.flux(0, 2)
+    step.side(3, 0)
+    settle(2, BACK_ROWS[2], own_ref, sem_br)
+    settle(3, BACK_ROWS[3], own_ref, sem_br)
+    finish(1, range(FIELDS))
+    for i in (2, 3):
+        step.flux(i, 0)
+    for i in (1, 2):
+        step.flux(i, 1)
+        step.flux(i, 2)
     for each in swaps:
         each.wait()
-    step.flux(0, 0)
-    step.flux(4, 0)
-    for i in (-1, 0, 3, 4):
-        step.flux(i, 1)
-        step.flux(i, 2)
-    settle(2, BACK_ROWS[2], own_ref, sem_br)
-    settle(3, BACK_ROWS[3], own_ref, sem_br)
-    for i in range(4):
+    for i in (2, 0, 3):
         finish(i, range(FIELDS))
     for part in range(PARTS):
         settle(part, OUT_ROWS[part], send_f, sem_fs)

time: 42.8 us -> 41.5 us (0.970)
  Pallas kernels: 42.1 us -> 40.7 us
    pallas_call x1, Pallas kernels: 40.3 us -> 39 us  [body(): pl.pallas_call(step_kernel, out_shape=shapes, in_specs=[hbm] * 5, out_spe...]
where the time goes in v3:
time: 41.5 us; the launch traced here: 41.4 us
  Pallas kernels  40.7 us (98%)
  between operations  0.64 us (2%)
    pallas_call x1, Pallas kernels, body(): pl.pallas_call(step_kernel, out_shape=shapes, in_specs=[hbm] * 5, out_spe...  39 us
    pallas_call x1, Pallas kernels, body(): pl.pallas_call(pass_kernel, out_shape=shapes, in_specs=[hbm] * 3, out_spe...  1.79 us

profile of v3, /device:TPU:1, one launch (start us, length us, event | category | flops | bytes accessed | tf_op | source)
XLA Modules:
  0.0 41.4 jit_solution(7215633085389454330)
XLA Ops:
  0.6 39.0 %step.1 = (f32[4,16,256]{2,1,0:T(8,128)}, f32[3,4,16,256]{3,2,1,0:T(8,128)}, f32[3,4,16,256]{3,2,1,0:T(8,128)}) custom-call(s32[4]{0:T(128)} %shift_hbm.1, f32[4]{0:T(128)} %frac_hbm.1, f32[4,16,256]{2,1,0:T(8,128)} %dens_hbm.1, f32[3,4,16,256]{3,2,1,0:T(8,128)} %mom_hbm.1, f32[3,4,16,256]{3,2,1,0:T(8,128)} %fld_hbm.1), custom_call_target="tpu_custom_call" | custom-call | tf_op jit(solution)/shard_map/step/pallas_call | solution.py:481
  39.6 1.8 %hand_on.1 = (f32[4,16,256]{2,1,0:T(8,128)}, f32[3,4,16,256]{3,2,1,0:T(8,128)}, f32[3,4,16,256]{3,2,1,0:T(8,128)}) custom-call(f32[4,16,256]{2,1,0:T(8,128)} %get-tuple-element.6.refs_0_, f32[3,4,16,256]{3,2,1,0:T(8,128)} %get-tuple-element.7.refs_1_, f32[3,4,16,256]{3,2,1,0:T(8,128)} %get-tuple-element.8.refs_2_), custom_call_target="tpu_custom_call" | custom-call | tf_op jit(solution)/shard_map/hand_on/pallas_call | solution.py:516

commit v4 on v3

--- a/solution.py
+++ b/solution.py
@@ -77,7 +77,7 @@
         )
         return carry
 
-    lax.fori_loop(0, PHI - 1, greet, 0)
+    lax.fori_loop(0, PHI - 1, greet, 0, unroll=True)
     pl.semaphore_signal(barrier, inc=1, device_id=above, device_id_type=MESH)
     pl.semaphore_signal(barrier, inc=1, device_id=below, device_id_type=MESH)
 
@@ -212,11 +212,13 @@
             each.start()
         return both
 
-    for fetch in fetches:
-        fetch.wait()
+    fetches[0].wait()
+    fetches[1].wait()
     arrange(0)
     pl.semaphore_wait(barrier, PHI - 1 + 2)
     send_out(0)
+    for fetch in fetches[2:]:
+        fetch.wait()
     arrange(1)
     send_out(1)
     arrange(2)
@@ -335,7 +337,11 @@
     return values
 
 
-def face_flux(low, high, normal, n, moved, wanted):
+def main(values):
+    return values[:, :, : 2 * LANES]
+
+
+def face_flux(low, high, normal, n, moved, wanted, narrow):
     square = normal * normal
 
     def fast(side, shifted):
@@ -343,27 +349,34 @@
 
     fastest = jnp.maximum(fast(low, moved), fast(high, same))
 
-    def blend(flux_low, flux_high, state_low, state_high):
-        return (flux_low + flux_high) - fastest * (state_high - state_low)
+    def blend(cut, flux, state):
+        parts = (flux(low), flux(high), state(low), state(high))
+        flux_low, flux_high, state_low, state_high = [
+            moved(cut(part)) if k % 2 == 0 else cut(part) for k, part in enumerate(parts)
+        ]
+        return (flux_low + flux_high) - cut(fastest) * (state_high - state_low)
+
+    def both(cut, value):
+        return cut(normal) * (moved(cut(value(low))) + cut(value(high)))
 
     result = {}
     if "m" in wanted:
-        result["m"] = [blend(moved(low["m"][n]), high["m"][n], moved(low["rho"]), high["rho"])]
+        cut = main if "m" in narrow else same
+        result["m"] = [blend(cut, lambda side: side["m"][n], lambda side: side["rho"])]
         for t in range(3):
             if t == n:
-                part = blend(moved(low["push"]), high["push"], moved(low["m"][n]), high["m"][n]) - square
+                part = blend(cut, lambda side: side["push"], lambda side: side["m"][n]) - cut(square)
             else:
                 part = blend(
-                    moved(low["m"][t] * low["v"][n]), high["m"][t] * high["v"][n],
-                    moved(low["m"][t]), high["m"][t],
-                ) - normal * (moved(low["b"][t]) + high["b"][t])
+                    cut, lambda side: side["m"][t] * side["v"][n], lambda side: side["m"][t]
+                ) - both(cut, lambda side: side["b"][t])
             result["m"].append(part)
     for t in range(3):
         if t in wanted:
+            cut = main if t in narrow else same
             result[t] = blend(
-                moved(low["b"][t] * low["v"][n]), high["b"][t] * high["v"][n],
-                moved(low["b"][t]), high["b"][t],
-            ) - normal * (moved(low["v"][t]) + high["v"][t])
+                cut, lambda side: side["b"][t] * side["v"][n], lambda side: side["b"][t]
+            ) - both(cut, lambda side: side["v"][t])
     return result
 
 
@@ -403,6 +416,8 @@
             cell = self.cell(i)
             t, u = [c for c in range(3) if c != n]
             b = {t: self.across(i, t), u: self.across(i, u)}
+            if n == 2 and i in (-1, 4):
+                cell, b = jax.tree.map(main, cell), jax.tree.map(main, b)
             square = b[t] * b[t] + b[u] * b[u]
             return dict(
                 cell, b=b, base=SOUND_SQUARED + square * cell["inv"], speed=jnp.abs(cell["v"][n]),
@@ -417,11 +432,11 @@
             normal = self.state(i)[4 + n]
             high = self.side(i, n)
             if n == 0:
-                return face_flux(self.side(i - 1, 0), high, normal, 0, same, ("m", 1, 2))
-            other = 3 - n
-            return face_flux(
-                high, high, normal, n, low_y if n == 1 else low_z, ("m", 0, other) if inner else (0,)
-            )
+                return face_flux(self.side(i - 1, 0), high, normal, 0, same, ("m", 1, 2), ("m", 2))
+            wanted = ("m", 0, 3 - n) if inner else (0,)
+            if n == 1:
+                return face_flux(high, high, normal, 1, low_y, wanted, ())
+            return face_flux(high, high, normal if inner else main(normal), 2, low_z, wanted, ("m", 0))
 
         return self.keep(("flux", i, n), make)
 
@@ -442,23 +457,24 @@
         step, edge_step = 0.5 * TIME_STEP, 0.125 * TIME_STEP
         if f < 4:
             y, z = self.flux(i, 1)["m"][f], self.flux(i, 2)["m"][f]
-            total = (self.flux(i + 1, 0)["m"][f] - self.flux(i, 0)["m"][f]) + (up_y(y) - y) + (up_z(z) - z)
-            new = self.state(i)[f] - step * total
+            total = self.flux(i + 1, 0)["m"][f] - self.flux(i, 0)["m"][f]
+            total = total + (main(up_y(y)) - main(y)) + (up_z(z) - z)
+            new = main(self.state(i)[f]) - step * total
             if f == 1:
-                new = new + TIME_STEP * 2.0 * ORBIT_FREQ * self.state(i)[2]
+                new = new + TIME_STEP * 2.0 * ORBIT_FREQ * main(self.state(i)[2])
             if f == 2:
-                new = new - TIME_STEP * (2.0 - SHEAR_RATE) * ORBIT_FREQ * self.state(i)[1]
+                new = new - TIME_STEP * (2.0 - SHEAR_RATE) * ORBIT_FREQ * main(self.state(i)[1])
             return new
         if f == 4:
             ez, ey = self.edge(i, 2), self.edge(i, 1)
-            curl = (up_y(ez) - ez) - (up_z(ey) - ey)
+            curl = (main(up_y(ez)) - main(ez)) - (up_z(ey) - ey)
         elif f == 5:
-            ex = self.edge(i, 0)
-            curl = (up_z(ex) - ex) - (self.edge(i + 1, 2) - self.edge(i, 2))
+            ex = main(self.edge(i, 0))
+            curl = (up_z(ex) - ex) - (main(self.edge(i + 1, 2)) - main(self.edge(i, 2)))
         else:
             ex = self.edge(i, 0)
-            curl = (self.edge(i + 1, 1) - self.edge(i, 1)) - (up_y(ex) - ex)
-        return self.state(i)[f] - edge_step * curl
+            curl = (self.edge(i + 1, 1) - self.edge(i, 1)) - (main(up_y(ex)) - main(ex))
+        return main(self.state(i)[f]) - edge_step * curl
 
 
 def pass_kernel(*refs):

time: 41.5 us -> 40.9 us (0.986)
  Pallas kernels: 40.7 us -> 40.2 us
    pallas_call x1, Pallas kernels: 39 us -> 38.4 us  [body(): pl.pallas_call(step_kernel, out_shape=shapes, in_specs=[hbm] * 5, out_spe...]
where the time goes in v4:
time: 40.9 us; the launch traced here: 40.8 us
  Pallas kernels  40.2 us (98%)
  between operations  0.64 us (2%)
    pallas_call x1, Pallas kernels, body(): pl.pallas_call(step_kernel, out_shape=shapes, in_specs=[hbm] * 5, out_spe...  38.4 us
    pallas_call x1, Pallas kernels, body(): pl.pallas_call(pass_kernel, out_shape=shapes, in_specs=[hbm] * 3, out_spe...  1.79 us

profile of v4, /device:TPU:1, one launch (start us, length us, event | category | flops | bytes accessed | tf_op | source)
XLA Modules:
  0.0 40.8 jit_solution(14880638410277711668)
XLA Ops:
  0.6 38.4 %step.1 = (f32[4,16,256]{2,1,0:T(8,128)}, f32[3,4,16,256]{3,2,1,0:T(8,128)}, f32[3,4,16,256]{3,2,1,0:T(8,128)}) custom-call(s32[4]{0:T(128)} %shift_hbm.1, f32[4]{0:T(128)} %frac_hbm.1, f32[4,16,256]{2,1,0:T(8,128)} %dens_hbm.1, f32[3,4,16,256]{3,2,1,0:T(8,128)} %mom_hbm.1, f32[3,4,16,256]{3,2,1,0:T(8,128)} %fld_hbm.1), custom_call_target="tpu_custom_call" | custom-call | tf_op jit(solution)/shard_map/step/pallas_call | solution.py:497
  39.0 1.8 %hand_on.1 = (f32[4,16,256]{2,1,0:T(8,128)}, f32[3,4,16,256]{3,2,1,0:T(8,128)}, f32[3,4,16,256]{3,2,1,0:T(8,128)}) custom-call(f32[4,16,256]{2,1,0:T(8,128)} %get-tuple-element.6.refs_0_, f32[3,4,16,256]{3,2,1,0:T(8,128)} %get-tuple-element.7.refs_1_, f32[3,4,16,256]{3,2,1,0:T(8,128)} %get-tuple-element.8.refs_2_), custom_call_target="tpu_custom_call" | custom-call | tf_op jit(solution)/shard_map/hand_on/pallas_call | solution.py:532

commit v5 on v4

--- a/solution.py
+++ b/solution.py
@@ -276,7 +276,7 @@
     step = Step(load, {1: load_one, 5: load_five})
     writes = []
 
-    def finish(i, fields):
+    def put(i, fields):
         for f in fields:
             values = step.result(f, i)
             for side in range(2):
@@ -284,16 +284,24 @@
                     weave[f, i, side, pl.ds(k, 8, stride=2), :] = values[
                         k, :, side * LANES:side * LANES + LANES
                     ]
+
+    def write(i, first, count, dst):
         for side in range(2):
             ys = pl.ds(side * LANES, LANES)
-            for src, dst in (
-                (weave.at[0, i, side], dens_out.at[i, :, ys]),
-                (weave.at[pl.ds(1, 3), i, side], mom_out.at[:, i, :, ys]),
-                (weave.at[pl.ds(4, 3), i, side], fld_out.at[:, i, :, ys]),
-            ):
-                write = pltpu.make_async_copy(src, dst, sem_out.at[len(writes)])
-                write.start()
-                writes.append(write)
+            src = weave.at[pl.ds(first, count), i, side] if count > 1 else weave.at[first, i, side]
+            copy = pltpu.make_async_copy(
+                src, dst.at[:, i, :, ys] if count > 1 else dst.at[i, :, ys], sem_out.at[len(writes)]
+            )
+            copy.start()
+            writes.append(copy)
+
+    def finish(i, fields=range(FIELDS)):
+        put(i, fields)
+        if 0 in fields:
+            write(i, 0, 1, dens_out)
+            write(i, 1, 3, mom_out)
+        if 6 in fields:
+            write(i, 4, 3, fld_out)
 
     step.flux(0, 1)
     step.flux(0, 2)
@@ -306,15 +314,17 @@
     for i in (1, 2):
         step.flux(i, 1)
         step.flux(i, 2)
+    finish(2, range(5))
     for each in swaps:
         each.wait()
-    for i in (2, 0, 3):
-        finish(i, range(FIELDS))
+    finish(0)
+    finish(3)
+    finish(2, (5, 6))
     for part in range(PARTS):
         settle(part, OUT_ROWS[part], send_f, sem_fs)
         settle(part, BACK_ROWS[part], send_b, sem_bs)
-    for write in writes:
-        write.wait()
+    for copy in writes:
+        copy.wait()
 
 
 def up_z(values):

time: 40.9 us -> 40.9 us (level)
  no operation moved by 1% of the time
where the time goes in v5:
time: 40.9 us; the launch traced here: 40.8 us
  Pallas kernels  40.1 us (98%)
  between operations  0.64 us (2%)
    pallas_call x1, Pallas kernels, body(): pl.pallas_call(step_kernel, out_shape=shapes, in_specs=[hbm] * 5, out_spe...  38.4 us
    pallas_call x1, Pallas kernels, body(): pl.pallas_call(pass_kernel, out_shape=shapes, in_specs=[hbm] * 3, out_spe...  1.79 us

profile of v5, /device:TPU:1, one launch (start us, length us, event | category | flops | bytes accessed | tf_op | source)
XLA Modules:
  0.0 40.8 jit_solution(8463502664117362129)
XLA Ops:
  0.6 38.4 %step.1 = (f32[4,16,256]{2,1,0:T(8,128)}, f32[3,4,16,256]{3,2,1,0:T(8,128)}, f32[3,4,16,256]{3,2,1,0:T(8,128)}) custom-call(s32[4]{0:T(128)} %shift_hbm.1, f32[4]{0:T(128)} %frac_hbm.1, f32[4,16,256]{2,1,0:T(8,128)} %dens_hbm.1, f32[3,4,16,256]{3,2,1,0:T(8,128)} %mom_hbm.1, f32[3,4,16,256]{3,2,1,0:T(8,128)} %fld_hbm.1), custom_call_target="tpu_custom_call" | custom-call | tf_op jit(solution)/shard_map/step/pallas_call | solution.py:507
  39.0 1.8 %hand_on.1 = (f32[4,16,256]{2,1,0:T(8,128)}, f32[3,4,16,256]{3,2,1,0:T(8,128)}, f32[3,4,16,256]{3,2,1,0:T(8,128)}) custom-call(f32[4,16,256]{2,1,0:T(8,128)} %get-tuple-element.6.refs_0_, f32[3,4,16,256]{3,2,1,0:T(8,128)} %get-tuple-element.7.refs_1_, f32[3,4,16,256]{3,2,1,0:T(8,128)} %get-tuple-element.8.refs_2_), custom_call_target="tpu_custom_call" | custom-call | tf_op jit(solution)/shard_map/hand_on/pallas_call | solution.py:542

commit v6 on v5

--- a/solution.py
+++ b/solution.py
@@ -65,10 +65,10 @@
     barrier = pltpu.get_barrier_semaphore()
 
     def partner(i):
-        k = i // 4
+        k = i % 16 // 2
         dz = 4 + (k + 1) // 2 * (1 - 2 * (k % 2))
         z = lax.rem(me // 2 + dz + 8, 8)
-        x = lax.rem(me // 16 + 1 - i // 2 % 2, 2)
+        x = lax.rem(me // 16 + 1 - i // 16, 2)
         return x * 16 + z * 2 + lax.rem(me + 1 - i % 2, 2)
 
     def greet(i, carry):

time: 40.9 us -> 40.3 us (0.985)
  Pallas kernels: 40.1 us -> 39.5 us
    pallas_call x1, Pallas kernels: 38.4 us -> 37.7 us  [body(): pl.pallas_call(step_kernel, out_shape=shapes, in_specs=[hbm] * 5, out_spe...]
where the time goes in v6:
time: 40.3 us; the launch traced here: 40.2 us
  Pallas kernels  39.5 us (98%)
  between operations  0.64 us (2%)
    pallas_call x1, Pallas kernels, body(): pl.pallas_call(step_kernel, out_shape=shapes, in_specs=[hbm] * 5, out_spe...  37.7 us
    pallas_call x1, Pallas kernels, body(): pl.pallas_call(pass_kernel, out_shape=shapes, in_specs=[hbm] * 3, out_spe...  1.79 us

profile of v6, /device:TPU:1, one launch (start us, length us, event | category | flops | bytes accessed | tf_op | source)
XLA Modules:
  0.0 40.2 jit_solution(9338907637083771073)
XLA Ops:
  0.6 37.7 %step.1 = (f32[4,16,256]{2,1,0:T(8,128)}, f32[3,4,16,256]{3,2,1,0:T(8,128)}, f32[3,4,16,256]{3,2,1,0:T(8,128)}) custom-call(s32[4]{0:T(128)} %shift_hbm.1, f32[4]{0:T(128)} %frac_hbm.1, f32[4,16,256]{2,1,0:T(8,128)} %dens_hbm.1, f32[3,4,16,256]{3,2,1,0:T(8,128)} %mom_hbm.1, f32[3,4,16,256]{3,2,1,0:T(8,128)} %fld_hbm.1), custom_call_target="tpu_custom_call" | custom-call | tf_op jit(solution)/shard_map/step/pallas_call | solution.py:507
  38.4 1.8 %hand_on.1 = (f32[4,16,256]{2,1,0:T(8,128)}, f32[3,4,16,256]{3,2,1,0:T(8,128)}, f32[3,4,16,256]{3,2,1,0:T(8,128)}) custom-call(f32[4,16,256]{2,1,0:T(8,128)} %get-tuple-element.6.refs_0_, f32[3,4,16,256]{3,2,1,0:T(8,128)} %get-tuple-element.7.refs_1_, f32[3,4,16,256]{3,2,1,0:T(8,128)} %get-tuple-element.8.refs_2_), custom_call_target="tpu_custom_call" | custom-call | tf_op jit(solution)/shard_map/hand_on/pallas_call | solution.py:542
